TPU v7x, 32 devices: a whole 2x2x4 slice. The times are simulated.
32 devices in a mesh: dom: 16 (over z, y, core), repl: 2 (over x).
Axes of the slice: x: 2, y: 2, z: 4, core: 2. Of those that a mesh axis runs over, the one named last changes fastest.
Arguments:
- features: float32 [16384, 256], P(('dom', 'repl')), may hold values from -6 to 6
- weight: bfloat16 [256, 256], replicated, may hold values from -0.375 to 0.375
- bias_vector: float32 [256], replicated, may hold values from -0.5 to 0.5
- cotangent: bfloat16 [16384, 256], P(('dom', 'repl')), may hold values from -6 to 6
- near_tiles: bfloat16 [128, 128, 128], P(('dom', 'repl')), may hold values from -0.3125 to 0.3125
- near_offsets: int32 [32, 9], P(('dom', 'repl')), may hold values from 0 to 4, as said below
- near_cols: int32 [32, 4], P(('dom', 'repl')), may hold values from 0 to 3, as said below
- far_tiles: bfloat16 [32, 16, 1, 128, 128], P(('dom', 'repl')), may hold values from -0.3125 to 0.3125
- far_rows: int32 [32, 16, 1], P(('dom', 'repl')), may hold values from -1 to 7, as said below
- far_cols: int32 [32, 16, 1], P(('dom', 'repl')), may hold values from 0 to 3
Outputs:
- hidden: bfloat16 [16384, 256], P(('dom', 'repl'))
- grad_features: float32 [16384, 256], P(('dom', 'repl'))
- weight_grad: float32 [256, 256], replicated
Inputs may be any that keep to these rules, and one draw needn't show every extreme that they name: `near_offsets`: each row is non-decreasing, begins with 0 and ends with 4. `near_cols`: within one tile row of one device the near tiles' columns differ and rise. `far_rows`: -1 marks an empty slot. A device's slots for the groups whose index of dom lies at most 1 step from its own around the cycle are never empty.
All inputs are finite; a program needn't handle non-finite values.
Results may differ from a plain program's by a relative error of at most 0.0075.
Values may be sent and summed in bfloat16 or wider, within the bound.
A program may use at most 128 MiB of HBM per device.

v0:
```python
import math

import jax
import jax.numpy as jnp
from jax import lax
from jax.sharding import PartitionSpec as P


def membership_flags(index, extent, dtype):
    return (index[..., None] == jnp.arange(extent, dtype=jnp.int32)).astype(dtype)


def slot_rows(offsets, slot_count):
    slots = jnp.arange(slot_count, dtype=jnp.int32)
    return jnp.sum((offsets[1:, None] <= slots[None, :]).astype(jnp.int32), axis=0)


def precise_total_sum(form, hot, values):
    return jnp.einsum(form, hot, values, precision=lax.Precision.HIGHEST)


def select(form, hot, values):
    return jnp.einsum(form, hot, values, preferred_element_type=jnp.float32).astype(jnp.bfloat16)


def tile_product(form, tiles, values):
    return jnp.einsum(form, tiles, values, preferred_element_type=jnp.float32)


def activation_grad(pre_values, upstream):
    sigma = jax.nn.sigmoid(pre_values)
    return (upstream.astype(jnp.float32) * sigma * (1.0 + pre_values * (1.0 - sigma))).astype(
        jnp.bfloat16
    )


def on_device(
    features,
    weight,
    bias_vector,
    cotangent,
    near_tiles,
    near_offsets,
    near_cols,
    far_tiles,
    far_rows,
    far_cols,
):
    rows_dev, feat_width = features.shape
    tile_size = near_tiles.shape[1]
    blocks_per_processor = rows_dev // tile_size
    dom_count = lax.axis_size("dom")
    repl_count = lax.axis_size("repl")
    blocks_dom = blocks_per_processor * repl_count
    near_count = near_tiles.shape[0]
    far_block = far_tiles[0]
    far_row_ids = far_rows[0]
    far_col_ids = far_cols[0]
    near_row_ids = slot_rows(near_offsets[0], near_count)
    nearby_column_index = near_cols[0]
    reduced = features.astype(jnp.bfloat16)
    local_block_list = reduced.reshape(blocks_per_processor, tile_size, feat_width)
    nearby_input_rows = select(
        "el,lxh->exh",
        membership_flags(nearby_column_index, blocks_per_processor, jnp.bfloat16),
        local_block_list,
    )
    near_prod = tile_product("qab,qbf->qaf", near_tiles, nearby_input_rows)
    partial_sum = precise_total_sum(
        "qr,qaf->raf", membership_flags(near_row_ids, blocks_dom, jnp.float32), near_prod
    )
    shard_rows = lax.all_gather(reduced, "dom", axis=0, tiled=True)
    range_count = shard_rows.shape[0] // rows_dev
    tiles = far_block
    row_ids = far_row_ids
    col_ids = far_col_ids
    source = shard_rows.reshape(range_count, blocks_per_processor, tile_size, feat_width)
    inputs = select(
        "kqc,kcbf->kqbf", membership_flags(col_ids, blocks_per_processor, jnp.bfloat16), source
    )
    far_prod = tile_product("kqab,kqbf->kqaf", tiles, inputs)
    partial_sum = partial_sum + precise_total_sum(
        "kqr,kqaf->raf", membership_flags(row_ids, blocks_dom, jnp.float32), far_prod
    )
    group_partial = partial_sum.reshape(blocks_dom * tile_size, feat_width)
    summed = lax.psum_scatter(group_partial, "repl", scatter_dimension=0, tiled=True).astype(
        jnp.bfloat16
    )
    pre_act = jnp.dot(summed, weight, preferred_element_type=jnp.float32) + bias_vector
    hidden = jax.nn.silu(pre_act).astype(jnp.bfloat16)
    grad_pre = activation_grad(pre_act, cotangent)
    weight_term = lax.dot_general(
        summed, grad_pre, (((0,), (0,)), ((), ())), preferred_element_type=jnp.float32
    )
    grad_rows = lax.dot_general(
        grad_pre, weight, (((1,), (1,)), ((), ())), preferred_element_type=jnp.float32
    ).astype(jnp.bfloat16)
    group_grad = lax.all_gather(grad_rows, "repl", axis=0, tiled=True)
    node_total = rows_dev * dom_count * repl_count
    weight_grad = lax.psum(weight_term, ("dom", "repl")) * (1.0 / math.sqrt(node_total))
    cluster_block_list = group_grad.reshape(blocks_dom, tile_size, feat_width)
    near_grads = select(
        "om,mgh->ogh", membership_flags(near_row_ids, blocks_dom, jnp.bfloat16), cluster_block_list
    )
    nearby_backward_pass = tile_product("ltp,ltk->lpk", near_tiles, near_grads)
    local_contribution = precise_total_sum(
        "ml,mrx->lrx",
        membership_flags(nearby_column_index, blocks_per_processor, jnp.float32),
        nearby_backward_pass,
    )
    row_count = rows_dev * lax.axis_size("dom")
    tiles = far_block
    row_ids = far_row_ids
    col_ids = far_col_ids
    far_grads = select(
        "kqr,rbf->kqbf", membership_flags(row_ids, blocks_dom, jnp.bfloat16), cluster_block_list
    )
    terms = tile_product("kqab,kqaf->kqbf", tiles, far_grads)
    placed = precise_total_sum(
        "kqc,kqbf->kcbf", membership_flags(col_ids, blocks_per_processor, jnp.float32), terms
    )
    far_grad = lax.psum_scatter(
        placed.reshape(row_count, feat_width).astype(jnp.bfloat16),
        "dom",
        scatter_dimension=0,
        tiled=True,
    ).astype(jnp.float32)
    grad_features = far_grad + local_contribution.reshape(rows_dev, feat_width)
    return (hidden, grad_features, weight_grad)


def solution(mesh):
    placed = (
        P(("dom", "repl"), None),
        P(),
        P(),
        P(("dom", "repl"), None),
        P(("dom", "repl"), None, None),
        P(("dom", "repl"), None),
        P(("dom", "repl"), None),
        P(("dom", "repl"), None, None, None, None),
        P(("dom", "repl"), None, None),
        P(("dom", "repl"), None, None),
    )
    return jax.shard_map(
        on_device,
        mesh=mesh,
        in_specs=placed,
        out_specs=(P(("dom", "repl"), None), P(("dom", "repl"), None), P()),
        check_vma=False,
    )
```

profile of v0, /device:TPU:0, one launch (start us, length us, event | category | flops | bytes accessed | tf_op | source)
XLA Modules:
  0.0 315.9 jit_solution(3008016414907530161)
XLA Ops:
  7.2 1.8 convert_element_type.53
  9.1 1.3 convolution_convert_fusion.3
  10.5 1.2 convolution_bitcast_fusion.3
  11.7 0.2 copy.20
  12.0 0.1 convert_reduce_fusion
  12.2 1.7 fusion.28
  13.9 50.2 %all-gather.2.cloned.1.call-done = bf16[8192,256]{1,0:T(8,128)(2,1)} async-done(((bf16[512,256]{1,0:T(8,128)(2,1)}), bf16[8192,256]{1,0:T(8,128)(2,1)}) %all-gather.2.cloned.1.call-update) | async-done | bytes 4194320 | tf_op jit(solution)/shard_map/all_gather | solution.py:72
  64.1 5.5 %fusion = bf16[16,1,128,256]{3,1,2,0:T(2,128)(2,1)S(1)} fusion(bf16[16,4,128,256]{3,2,1,0:T(8,128)(2,1)} %bitcast.66, pred[16,4,1,1]{1,0,2,3:T(8,128)(4,1)S(1)} %get-tuple-element.6), kind=kOutput, calls=%fused_computation.1 | convolution fusion | flops 4194304 | bytes 5242944 | tf_op jit(solution)/shard_map/kqc,kcbf->kqbf/dot_general | solution.py:23
  69.6 3.4 %copy.33 = bf16[16,1,128,256]{2,3,0,1:T(8,128)(2,1)} copy(bf16[16,1,128,256]{3,1,2,0:T(2,128)(2,1)S(1)} %fusion) | data formatting | bytes 2097152 | tf_op jit(solution)/shard_map/kqc,kcbf->kqbf/dot_general | solution.py:23
  72.9 1.7 convolution_bitcast_fusion.1
  74.6 2.1 copy.21
  76.7 2.7 convolution_add_fusion
  79.4 1.3 copy.22
  80.8 18.9 %reduce-scatter.3.cloned.1.call-done = f32[512,256]{1,0:T(8,128)} async-done(((f32[1024,256]{1,0:T(8,128)}), f32[512,256]{1,0:T(8,128)}) %reduce-scatter.3.cloned.1.call-update) | async-done | bytes 524304 | tf_op jit(solution)/shard_map/reduce_scatter | solution.py:86
  99.7 2.2 multiply_convert_fusion.1
  101.9 0.3 convolution_convert_fusion.2
  102.2 1.0 fusion.10
  103.2 8.9 %all_gather.7 = bf16[1024,256]{1,0:T(8,128)(2,1)S(1)} all-gather(bf16[512,256]{1,0:T(8,128)(2,1)S(1)} %convolution_convert_fusion.2), channel_id=1, replica_groups=mesh['dom'=16,'repl'=2] {'repl'}, dimensions={0}, use_global_device_ids=true | all-gather | bytes 786432 | tf_op jit(solution)/shard_map/all_gather | solution.py:98
  112.1 0.5 convolution_convert_fusion
  112.6 0.5 convolution_bitcast_fusion
  113.2 1.8 copy.25
  115.0 5.1 %multiply_convert_fusion = bf16[16,4,128,256]{3,2,1,0:T(8,128)(2,1)} fusion(f32[16,128,256]{2,1,0:T(8,128)} %copy.25, f32[16,4]{1,0:T(8,128)S(1)} %get-tuple-element.5), kind=kLoop, calls=%fused_computation | loop fusion | flops 4194304 | bytes 6291712 | tf_op jit(solution)/shard_map/convert_element_type | solution.py:123
  120.2 0.4 convolution_convert_fusion.1
  120.6 0.4 copy-done.1
  121.0 0.3 convolution_bitcast_fusion.2
  121.3 0.2 copy.28
  121.6 0.6 fusion.24
  122.2 0.1 copy.29
  122.3 109.4 %all-reduce.2.cloned.1.call-done = f32[256,256]{1,0:T(8,128)} async-done(((f32[256,256]{1,0:T(8,128)}), f32[256,256]{1,0:T(8,128)}) %all-reduce.2.cloned.1.call-update) | async-done | bytes 262160 | tf_op jit(solution)/shard_map/psum | solution.py:100
  231.7 1.7 broadcast_multiply_fusion
  233.3 74.3 %reduce-scatter.5.cloned.1.call-done = bf16[512,256]{1,0:T(8,128)(2,1)} async-done(((bf16[8192,256]{1,0:T(8,128)(2,1)}), bf16[512,256]{1,0:T(8,128)(2,1)}) %reduce-scatter.5.cloned.1.call-update) | async-done | bytes 262160 | tf_op jit(solution)/shard_map/reduce_scatter | solution.py:122
  307.6 1.8 bitcast_add_fusion
  (29 shorter events, 0.4 us)
Async XLA Ops:
  7.2 65.8 %copy-start = (bf16[1,16,1,128,128]{4,3,2,1,0:T(8,128)(2,1)S(1)}, bf16[1,16,1,128,128]{4,3,2,1,0:T(8,128)(2,1)}, u32[]{:S(2)}) copy-start(bf16[1,16,1,128,128]{4,3,2,1,0:T(8,128)(2,1)} %param.17) | copy-start | bytes 1572868
  7.2 4.7 %copy-start.9 = (s32[1,9]{1,0:T(1,128)S(1)}, s32[1,9]{1,0:T(1,128)}, u32[]{:S(2)}) copy-start(s32[1,9]{1,0:T(1,128)} %param.15) | copy-start | bytes 112
  7.2 4.9 %copy-start.6 = (s32[1,16,1]{1,2,0:T(1,128)S(1)}, s32[1,16,1]{1,2,0:T(1,128)}, u32[]{:S(2)}) copy-start(s32[1,16,1]{1,2,0:T(1,128)} %param.19) | copy-start | bytes 196
  7.2 56.9 %all-gather.2.cloned.1.call-start = ((), (), s32[]{:S(2)}) async-start(), calls=%async_computation.2 | async-start | bytes 4456448 | tf_op jit(solution)/shard_map/all_gather | solution.py:72
  9.1 90.6 %reduce-scatter.3.cloned.1.call-start = ((), (), s32[]{:S(2)}) async-start(), calls=%async_computation.3 | async-start | bytes 1572864 | tf_op jit(solution)/shard_map/reduce_scatter | solution.py:86
  74.6 2.1 copy-start.4
  79.3 20.3 %copy-start.3 = (bf16[256,256]{1,0:T(8,128)(2,1)S(1)}, bf16[256,256]{1,0:T(8,128)(2,1)}, u32[]{:S(2)}) copy-start(bf16[256,256]{1,0:T(8,128)(2,1)} %param.11) | copy-start | bytes 393220
  79.4 20.3 %copy-start.7 = (bf16[512,256]{1,0:T(8,128)(2,1)S(1)}, bf16[512,256]{1,0:T(8,128)(2,1)}, u32[]{:S(2)}) copy-start(bf16[512,256]{1,0:T(8,128)(2,1)} %param.13) | copy-start | bytes 786436
  79.4 20.3 %copy-start.8 = (f32[256]{0:T(256)S(1)}, f32[256]{0:T(256)}, u32[]{:S(2)}) copy-start(f32[256]{0:T(256)} %param.12) | copy-start | bytes 3076
  80.7 151.0 %all-reduce.2.cloned.1.call-start = ((), (), s32[]{:S(2)}) async-start(), calls=%async_computation.5 | async-start | bytes 524288 | tf_op jit(solution)/shard_map/psum | solution.py:100
  99.7 2.5 copy-start.2
  103.2 204.4 %reduce-scatter.5.cloned.1.call-start = ((), (), s32[]{:S(2)}) async-start(), calls=%async_computation.4 | async-start | bytes 4456448 | tf_op jit(solution)/shard_map/reduce_scatter | solution.py:122
  120.1 0.9 copy-start.1
  120.2 1.4 copy-start.5
Sparse Core Ops, SparseCore 0:
  10.8 53.2 all-gather.1
  80.8 18.7 reduce-scatter.2
  106.7 124.9 all-reduce.1
  235.9 71.6 reduce-scatter.4
where the time goes:
time: 316 us
  waiting for transfers between devices  253 us (80%)
  matrix products  19.9 us (6%)
  between operations  14 us (4%)
  other arithmetic  10.6 us (3%)
  local copies, waits for them, and re-layouts  9.66 us (3%)
  blocking collectives  8.9 us (3%)
    psum x1, waiting for transfers between devices, on_device(): lax.psum(weight_term, ('dom', 'repl')) * (1.0 / math.sqrt(node_total))  109 us
    reduce_scatter x1, waiting for transfers between devices, on_device(): lax.psum_scatter(placed.reshape(row_count, feat_width).astype(jnp.bfloat1...  74.3 us
    all_gather x1, waiting for transfers between devices, on_device(): shard_rows = lax.all_gather(reduced, 'dom', axis=0, tiled=True)  50.2 us
    reduce_scatter x1, waiting for transfers between devices, on_device(): lax.psum_scatter(group_partial, 'repl', scatter_dimension=0, tiled=True)  18.9 us
    all_gather x1, blocking collectives, on_device(): group_grad = lax.all_gather(grad_rows, 'repl', axis=0, tiled=True)  8.9 us
    dot_general x4, matrix products, select(): jnp.einsum(form, hot, values, preferred_element_type=jnp.float32)  7.78 us
  transfers between devices with their start and end apart: 4, of which 4 were waited for; matrix products, arithmetic and copies ran while one was open for 5% of the time, Pallas kernels for 0%

commit v1 on v0

--- a/solution.py
+++ b/solution.py
@@ -1,8 +1,11 @@
+import functools
 import math
 
 import jax
 import jax.numpy as jnp
 from jax import lax
+from jax.experimental import pallas as pl
+from jax.experimental.pallas import tpu as pltpu
 from jax.sharding import PartitionSpec as P
 
 
@@ -129,6 +132,467 @@
     return (hidden, grad_features, weight_grad)
 
 
+MESH = pl.DeviceIdType.MESH
+FAST_PLANE = 4
+
+
+def remote(src, dst, send_sem, recv_sem, dom, repl):
+    return pltpu.make_async_remote_copy(
+        src_ref=src,
+        dst_ref=dst,
+        send_sem=send_sem,
+        recv_sem=recv_sem,
+        device_id=(dom, repl),
+        device_id_type=MESH,
+    )
+
+
+def layer_kernel(
+    dom_count,
+    near_count,
+    scale,
+    flags,
+    features,
+    weight,
+    bias,
+    cotangent,
+    near_tiles,
+    far_tiles,
+    hidden,
+    grad_features,
+    weight_grad,
+    own_feats,
+    col_out,
+    col_in,
+    feat_out,
+    feat_in,
+    dense,
+    far_flip,
+    near_flip,
+    part_out,
+    part_in,
+    part_own,
+    summed,
+    grad_pre,
+    group_grad,
+    term_out,
+    term_in,
+    share_out,
+    share_in,
+    plane_sum,
+    final_share,
+    col_send,
+    col_recv,
+    feat_send,
+    feat_recv,
+    part_send,
+    part_recv,
+    grad_send,
+    grad_recv,
+    term_send,
+    term_recv,
+    share_send,
+    share_recv,
+    plane_send,
+    plane_recv,
+    final_send,
+    final_recv,
+):
+    f32, bf16 = jnp.float32, jnp.bfloat16
+    dom, repl = lax.axis_index("dom"), lax.axis_index("repl")
+    other = 1 - repl
+    planes = dom_count // FAST_PLANE
+    plane, lane = dom // FAST_PLANE, dom % FAST_PLANE
+    rows_dev, feat = features.shape
+    tile = near_tiles.shape[1]
+    half = feat // 2
+    blocks = rows_dev // tile
+    rows_dom = 2 * blocks
+    near_cols_at = near_count * rows_dom
+    far_rows_at = near_cols_at + near_count * blocks
+    far_cols_at = far_rows_at + dom_count * rows_dom
+
+    def near_row(q, r):
+        return flags[q * rows_dom + r]
+
+    def near_col(q, c):
+        return flags[near_cols_at + q * blocks + c]
+
+    def far_row(k, r):
+        return flags[far_rows_at + k * rows_dom + r]
+
+    def far_col(k, c):
+        return flags[far_cols_at + k * blocks + c]
+
+    def at_distance(a, b):
+        return ((plane + a) % planes) * FAST_PLANE + (lane + b) % FAST_PLANE
+
+    steps = [(a, b) for a in (2, 3, 1, 0) for b in range(FAST_PLANE) if (a, b) != (0, 0)]
+    steps = [(a, b) for a, b in steps if a < planes]
+    mates = [(b, c) for b in range(FAST_PLANE) for c in range(2) if (b, c) != (0, 0)]
+
+    def mate(b, c):
+        return plane * FAST_PLANE + (lane + b) % FAST_PLANE, (repl + c) % 2
+
+    barrier = pltpu.get_barrier_semaphore()
+    for a, b in steps:
+        pl.semaphore_signal(barrier, inc=1, device_id=(at_distance(a, b), repl), device_id_type=MESH)
+    for b in range(FAST_PLANE):
+        pl.semaphore_signal(barrier, inc=1, device_id=mate(b, 1), device_id_type=MESH)
+    col_out[...] = jnp.zeros_like(col_out)
+    for k in range(dom_count):
+        for c in range(blocks):
+            col_out[k, c : c + 1] = jnp.full((1, half), far_col(k, c), f32)
+    col_in[dom] = col_out[dom]
+    for h in range(2):
+        own_feats[h] = features[:, h * half : (h + 1) * half].astype(bf16)
+    pl.semaphore_wait(barrier, len(steps) + FAST_PLANE)
+
+    def col_copy(i, peer):
+        return remote(
+            col_out.at[peer], col_in.at[dom], col_send.at[i], col_recv.at[i], peer, repl
+        )
+
+    def source(i):
+        a, b = steps[i]
+        return at_distance((planes - a) % planes, (FAST_PLANE - b) % FAST_PLANE)
+
+    for i, (a, b) in enumerate(steps):
+        col_copy(i, at_distance(a, b)).start()
+
+    def chosen(k, h):
+        want = col_in[k]
+        pick = jnp.zeros((tile, half), f32)
+        for c in range(blocks):
+            block = features[c * tile : (c + 1) * tile, h * half : (h + 1) * half]
+            pick = pick + block * want[c : c + 1]
+        return pick.astype(bf16)
+
+    def feat_copy(h, i, peer):
+        return remote(
+            feat_out.at[h, i],
+            feat_in.at[h, pl.ds(pl.multiple_of(dom * tile, tile), tile)],
+            feat_send.at[h, i],
+            feat_recv.at[h, i],
+            peer,
+            repl,
+        )
+
+    opposite = {}
+    for i, (a, b) in enumerate(steps):
+        opposite[i] = steps.index(((planes - a) % planes, (FAST_PLANE - b) % FAST_PLANE))
+    for h in range(2):
+        for i, (a, b) in enumerate(steps):
+            peer = at_distance(a, b)
+            if h == 0:
+                col_copy(opposite[i], peer).wait_recv()
+            feat_out[h, i] = chosen(peer, h)
+            feat_copy(h, i, peer).start()
+    for h in range(2):
+        feat_in[h, pl.ds(pl.multiple_of(dom * tile, tile), tile)] = chosen(dom, h)
+
+    for q in range(near_count):
+        near_flip[q] = near_tiles[q].astype(f32).T.astype(bf16)
+    for r in range(rows_dom):
+        for c in range(blocks):
+            block = jnp.zeros((tile, tile), f32)
+            for q in range(near_count):
+                block = block + near_tiles[q].astype(f32) * (near_row(q, r) * near_col(q, c))
+            dense[r * tile : (r + 1) * tile, c * tile : (c + 1) * tile] = block.astype(bf16)
+
+    def build(k, carry):
+        block = far_tiles[k].astype(f32)
+        far_flip[k] = block.T.astype(bf16)
+        at = pl.ds(pl.multiple_of(rows_dev + k * tile, tile), tile)
+        for r in range(rows_dom):
+            dense[r * tile : (r + 1) * tile, at] = (block * far_row(k, r)).astype(bf16)
+        return carry
+
+    lax.fori_loop(0, dom_count, build, 0)
+
+    def aggregate(owner, h):
+        at = pl.ds(pl.multiple_of(owner * rows_dev, rows_dev), rows_dev)
+        return jnp.dot(dense[at, :rows_dev], own_feats[h], preferred_element_type=f32) + jnp.dot(
+            dense[at, rows_dev:], feat_in[h], preferred_element_type=f32
+        )
+
+    def part_copy(h):
+        return remote(
+            part_out.at[h], part_in.at[h], part_send.at[h], part_recv.at[h], dom, other
+        )
+
+    for h in range(2):
+        for i, (a, b) in enumerate(steps):
+            feat_copy(h, i, at_distance(a, b)).wait_recv()
+        part_out[h] = aggregate(other, h).astype(bf16)
+        part_copy(h).start()
+        part_own[h] = aggregate(repl, h)
+    for h in range(2):
+        part_copy(h).wait_recv()
+        summed[:, h * half : (h + 1) * half] = (part_own[h] + part_in[h].astype(f32)).astype(bf16)
+
+    pre_act = jnp.dot(summed[...], weight[...], preferred_element_type=f32) + bias[...]
+    sigma = 1.0 / (1.0 + jnp.exp(-pre_act))
+    hidden[...] = (pre_act * sigma).astype(bf16)
+    grad_pre[...] = (
+        cotangent[...].astype(f32) * sigma * (1.0 + pre_act * (1.0 - sigma))
+    ).astype(bf16)
+
+    mine = pl.ds(pl.multiple_of(repl * rows_dev, rows_dev), rows_dev)
+
+    def grad_copy(h):
+        return remote(
+            group_grad.at[h, mine],
+            group_grad.at[h, mine],
+            grad_send.at[h],
+            grad_recv.at[h],
+            dom,
+            other,
+        )
+
+    for h in range(2):
+        group_grad[h, mine] = lax.dot_general(
+            grad_pre[...],
+            weight[h * half : (h + 1) * half, :],
+            (((1,), (1,)), ((), ())),
+            preferred_element_type=f32,
+        ).astype(bf16)
+        grad_copy(h).start()
+
+    place = lane * 2 + repl
+    shares = 2 * FAST_PLANE
+    share_rows = feat // shares
+    for p in range(shares):
+        share_out[p] = lax.dot_general(
+            summed[:, p * share_rows : (p + 1) * share_rows],
+            grad_pre[...],
+            (((0,), (0,)), ((), ())),
+            preferred_element_type=f32,
+        ).astype(bf16)
+    share_in[place] = share_out[place]
+
+    def share_copy(i):
+        to_dom, to_repl = mate(*mates[i])
+        return remote(
+            share_out.at[(to_dom % FAST_PLANE) * 2 + to_repl],
+            share_in.at[place],
+            share_send.at[i],
+            share_recv.at[i],
+            to_dom,
+            to_repl,
+        )
+
+    for i in range(len(mates)):
+        share_copy(i).start()
+
+    def far_term(k, h):
+        rows = jnp.zeros((tile, half), f32)
+        for r in range(rows_dom):
+            rows = rows + group_grad[h, r * tile : (r + 1) * tile].astype(f32) * far_row(k, r)
+        return jnp.dot(far_flip[k], rows.astype(bf16), preferred_element_type=f32)
+
+    def term_copy(h, i, peer):
+        return remote(
+            term_out.at[h, i], term_in.at[h, dom], term_send.at[h, i], term_recv.at[h, i], peer, repl
+        )
+
+    for h in range(2):
+        grad_copy(h).wait_recv()
+        for i, (a, b) in enumerate(steps):
+            peer = at_distance(a, b)
+            term_out[h, i] = far_term(peer, h).astype(bf16)
+            term_copy(h, i, peer).start()
+        term_in[h, dom] = far_term(dom, h).astype(bf16)
+
+    for i in range(len(mates)):
+        share_copy(i).wait_recv()
+    total = share_in[0].astype(f32)
+    for p in range(1, shares):
+        total = total + share_in[p].astype(f32)
+    plane_sum[plane] = total.astype(bf16)
+
+    def plane_copy(a):
+        return remote(
+            plane_sum.at[plane],
+            plane_sum.at[plane],
+            plane_send.at[a - 1],
+            plane_recv.at[a - 1],
+            at_distance(a, 0),
+            repl,
+        )
+
+    for a in range(1, planes):
+        plane_copy(a).start()
+
+    for h in range(2):
+        at = slice(h * half, (h + 1) * half)
+        near_terms = []
+        for q in range(near_count):
+            rows = jnp.zeros((tile, half), f32)
+            for r in range(rows_dom):
+                rows = rows + group_grad[h, r * tile : (r + 1) * tile].astype(f32) * near_row(q, r)
+            near_terms.append(jnp.dot(near_flip[q], rows.astype(bf16), preferred_element_type=f32))
+        for c in range(blocks):
+            block = jnp.zeros((tile, half), f32)
+            for q in range(near_count):
+                block = block + near_terms[q] * near_col(q, c)
+            grad_features[c * tile : (c + 1) * tile, at] = block
+
+    for a in range(1, planes):
+        plane_copy(a).wait_recv()
+    total = plane_sum[0].astype(f32)
+    for z in range(1, planes):
+        total = total + plane_sum[z].astype(f32)
+    final_share[place] = total * scale
+
+    def final_copy(i):
+        to_dom, to_repl = mate(*mates[i])
+        return remote(
+            final_share.at[place],
+            final_share.at[place],
+            final_send.at[i],
+            final_recv.at[i],
+            to_dom,
+            to_repl,
+        )
+
+    for i in range(len(mates)):
+        final_copy(i).start()
+
+    def place_term(k, h):
+        at = slice(h * half, (h + 1) * half)
+        want = col_in[k]
+        term = term_in[h, k].astype(f32)
+        for c in range(blocks):
+            rows = slice(c * tile, (c + 1) * tile)
+            grad_features[rows, at] += term * want[c : c + 1]
+
+    for h in range(2):
+        place_term(dom, h)
+        for i in range(len(steps)):
+            term_copy(h, i, at_distance(*steps[i])).wait_recv()
+            place_term(source(i), h)
+
+    for i in range(len(mates)):
+        final_copy(i).wait_recv()
+    for p in range(shares):
+        weight_grad[p * share_rows : (p + 1) * share_rows, :] = final_share[p]
+
+    for i, (a, b) in enumerate(steps):
+        peer = at_distance(a, b)
+        col_copy(i, peer).wait_send()
+        for h in range(2):
+            feat_copy(h, i, peer).wait_send()
+            term_copy(h, i, peer).wait_send()
+    for h in range(2):
+        part_copy(h).wait_send()
+        grad_copy(h).wait_send()
+    for i in range(len(mates)):
+        share_copy(i).wait_send()
+        final_copy(i).wait_send()
+    for a in range(1, planes):
+        plane_copy(a).wait_send()
+
+
+def fused_on_device(
+    features,
+    weight,
+    bias_vector,
+    cotangent,
+    near_tiles,
+    near_offsets,
+    near_cols,
+    far_tiles,
+    far_rows,
+    far_cols,
+):
+    rows_dev, feat = features.shape
+    tile = near_tiles.shape[1]
+    near_count = near_tiles.shape[0]
+    dom_count = lax.axis_size("dom")
+    half = feat // 2
+    peers = dom_count - 1
+    shares = 2 * FAST_PLANE
+    mates = shares - 1
+    planes = dom_count // FAST_PLANE
+    blocks = rows_dev // tile
+    near_rows = slot_rows(near_offsets[0], near_count)
+    hot = (
+        membership_flags(near_rows, 2 * blocks, jnp.float32),
+        membership_flags(near_cols[0], blocks, jnp.float32),
+        membership_flags(far_rows.reshape(-1), 2 * blocks, jnp.float32),
+        membership_flags(far_cols.reshape(-1), blocks, jnp.float32),
+    )
+    flags = jnp.concatenate([part.reshape(-1) for part in hot])
+    scale = 1.0 / math.sqrt(rows_dev * dom_count * 2)
+    bf16, f32 = jnp.bfloat16, jnp.float32
+    vmem = pl.BlockSpec(memory_space=pltpu.VMEM)
+    dma = pltpu.SemaphoreType.DMA
+    return pl.pallas_call(
+        functools.partial(layer_kernel, dom_count, near_count, scale),
+        out_shape=(
+            jax.ShapeDtypeStruct((rows_dev, feat), bf16),
+            jax.ShapeDtypeStruct((rows_dev, feat), f32),
+            jax.ShapeDtypeStruct((feat, feat), f32),
+        ),
+        in_specs=[pl.BlockSpec(memory_space=pltpu.SMEM)] + [vmem] * 6,
+        out_specs=(vmem, vmem, vmem),
+        scratch_shapes=[
+            pltpu.VMEM((2, rows_dev, half), bf16),
+            pltpu.VMEM((dom_count, 8, half), f32),
+            pltpu.VMEM((dom_count, 8, half), f32),
+            pltpu.VMEM((2, peers, tile, half), bf16),
+            pltpu.VMEM((2, dom_count * tile, half), bf16),
+            pltpu.VMEM((2 * rows_dev, rows_dev + dom_count * tile), bf16),
+            pltpu.VMEM((dom_count, tile, tile), bf16),
+            pltpu.VMEM((near_count, tile, tile), bf16),
+            pltpu.VMEM((2, rows_dev, half), bf16),
+            pltpu.VMEM((2, rows_dev, half), bf16),
+            pltpu.VMEM((2, rows_dev, half), f32),
+            pltpu.VMEM((rows_dev, feat), bf16),
+            pltpu.VMEM((rows_dev, feat), bf16),
+            pltpu.VMEM((2, 2 * rows_dev, half), bf16),
+            pltpu.VMEM((2, peers, tile, half), bf16),
+            pltpu.VMEM((2, dom_count, tile, half), bf16),
+            pltpu.VMEM((shares, feat // shares, feat), bf16),
+            pltpu.VMEM((shares, feat // shares, feat), bf16),
+            pltpu.VMEM((planes, feat // shares, feat), bf16),
+            pltpu.VMEM((shares, feat // shares, feat), f32),
+            dma((peers,)),
+            dma((peers,)),
+            dma((2, peers)),
+            dma((2, peers)),
+            dma((2,)),
+            dma((2,)),
+            dma((2,)),
+            dma((2,)),
+            dma((2, peers)),
+            dma((2, peers)),
+            dma((mates,)),
+            dma((mates,)),
+            dma((planes - 1,)),
+            dma((planes - 1,)),
+            dma((mates,)),
+            dma((mates,)),
+        ],
+        compiler_params=pltpu.CompilerParams(
+            collective_id=0, has_side_effects=True, vmem_limit_bytes=40 * 1024 * 1024
+        ),
+    )(
+        flags,
+        features,
+        weight,
+        bias_vector.reshape(1, feat),
+        cotangent,
+        near_tiles,
+        far_tiles.reshape(dom_count, tile, tile),
+    )
+
+
+def fits_one_kernel(mesh):
+    return mesh.shape["repl"] == 2 and mesh.shape["dom"] == 4 * FAST_PLANE
+
+
 def solution(mesh):
     placed = (
         P(("dom", "repl"), None),
@@ -143,7 +607,7 @@
         P(("dom", "repl"), None, None),
     )
     return jax.shard_map(
-        on_device,
+        fused_on_device if fits_one_kernel(mesh) else on_device,
         mesh=mesh,
         in_specs=placed,
         out_specs=(P(("dom", "repl"), None), P(("dom", "repl"), None), P()),

time: 316 us -> 87 us (0.28)
  waiting for transfers between devices: 253 us -> 0 us
  Pallas kernels: 0 us -> 75 us
  matrix products: 19.9 us -> 0 us
  between operations: 14 us -> 0.67 us
  other arithmetic: 10.6 us -> 0.49 us
  blocking collectives: 8.9 us -> 0 us
    psum x1 -> x0, waiting for transfers between devices: 109 us -> none  [on_device(): lax.psum(weight_term, ('dom', 'repl')) * (1.0 / math.sqrt(node_total))]
    reduce_scatter x2 -> x0, waiting for transfers between devices: 93.2 us -> none  [the longest x1 74.3 us: on_device(): lax.psum_scatter(placed.reshape(row_count, feat_width).astype(jnp.bfloat1...]
    pallas_call x0 -> x1, Pallas kernels: none -> 75 us  [fused_on_device(): pl.pallas_call(functools.partial(layer_kernel, dom_count, near_count, sca...]
    all_gather x1 -> x0, waiting for transfers between devices: 50.2 us -> none  [on_device(): shard_rows = lax.all_gather(reduced, 'dom', axis=0, tiled=True)]
    dot_general x14 -> x0, matrix products: 19.9 us -> none  [the longest x4 7.78 us: select(): jnp.einsum(form, hot, values, preferred_element_type=jnp.float32)]
    unnamed x20 -> x23, local copies, waits for them, and re-layouts: 0.48 us -> 9.98 us
    all_gather x1 -> x0, blocking collectives: 8.9 us -> none  [on_device(): group_grad = lax.all_gather(grad_rows, 'repl', axis=0, tiled=True)]
    dot_general x6 -> x0, local copies, waits for them, and re-layouts: 7.81 us -> none  [the longest x4 4.35 us: tile_product(): return jnp.einsum(form, tiles, values, preferred_element_type=jnp.float32)]
  transfers between devices with their start and end apart: 4 -> 0, of which waited for: 4 -> 0; matrix products, arithmetic and copies ran while one was open for 5% -> 0% of each run, Pallas kernels for 0% -> 0%
where the time goes in v1:
time: 87 us; the launch traced here: 86.6 us
  Pallas kernels  75 us (86%)
  local copies, waits for them, and re-layouts  10.4 us (12%)
    pallas_call x1, Pallas kernels, fused_on_device(): pl.pallas_call(functools.partial(layer_kernel, dom_count, near_count, sca...  75 us
    unnamed x23, local copies, waits for them, and re-layouts  9.98 us

profile of v1, /device:TPU:0, one launch (start us, length us, event | category | flops | bytes accessed | tf_op | source)
XLA Modules:
  0.0 86.6 jit_solution(17416964036322444928)
XLA Ops:
  0.6 0.0 copy-start.8
  0.6 0.6 copy-done.8
  1.3 0.1 slice_bitcast_fusion
  1.4 0.1 convert_reduce_fusion
  1.5 0.1 iota_compare_fusion.3
  1.6 0.0 copy-start.9
  1.6 0.1 convert_element_type.24
  1.6 0.6 copy-done.9
  2.2 0.1 iota_compare_fusion.2
  2.3 0.0 copy-start.6
  2.3 0.1 convert_element_type.25
  2.4 0.6 copy-done.6
  2.9 0.1 iota_compare_fusion.1
  3.0 0.0 copy-start.7
  3.0 0.1 convert_element_type.26
  3.1 0.6 copy-done.7
  3.7 0.1 iota_compare_fusion
  3.7 0.1 convert_element_type.27
  3.8 0.0 copy-start.5
  3.9 0.1 add_convert_fusion.flags
  3.9 0.6 copy-done.5
  4.5 0.0 copy-start
  4.5 1.0 %copy-done = f32[512,256]{1,0:T(8,128)S(1)} copy-done((f32[512,256]{1,0:T(8,128)S(1)}, f32[512,256]{1,0:T(8,128)}, u32[]{:S(2)}) %copy-start) | copy-done | bytes 524312
  5.6 0.0 copy-start.1
  5.6 1.0 %copy-done.1 = bf16[1,16,1,128,128]{4,3,2,1,0:T(8,128)(2,1)S(1)} copy-done((bf16[1,16,1,128,128]{4,3,2,1,0:T(8,128)(2,1)S(1)}, bf16[1,16,1,128,128]{4,3,2,1,0:T(8,128)(2,1)}, u32[]{:S(2)}) %copy-start.1) | copy-done | bytes 524312
  6.6 0.9 %copy-done.2 = bf16[512,256]{1,0:T(8,128)(2,1)S(1)} copy-done((bf16[512,256]{1,0:T(8,128)(2,1)S(1)}, bf16[512,256]{1,0:T(8,128)(2,1)}, u32[]{:S(2)}) %copy-start.2) | copy-done | bytes 262168
  7.6 0.9 %copy-done.3 = bf16[256,256]{1,0:T(8,128)(2,1)S(1)} copy-done((bf16[256,256]{1,0:T(8,128)(2,1)S(1)}, bf16[256,256]{1,0:T(8,128)(2,1)}, u32[]{:S(2)}) %copy-start.3) | copy-done | bytes 131096
  8.5 0.9 %copy-done.4 = bf16[4,128,128]{2,1,0:T(8,128)(2,1)S(1)} copy-done((bf16[4,128,128]{2,1,0:T(8,128)(2,1)S(1)}, bf16[4,128,128]{2,1,0:T(8,128)(2,1)}, u32[]{:S(2)}) %copy-start.4) | copy-done | bytes 131096
  9.4 75.0 %shard_map.121 = (bf16[512,256]{1,0:T(8,128)(2,1)S(1)}, f32[512,256]{1,0:T(8,128)S(1)}, f32[256,256]{1,0:T(8,128)S(1)}) custom-call(f32[240]{0:T(256)S(1)} %add_convert_fusion.flags, f32[512,256]{1,0:T(8,128)S(1)} %copy-done, bf16[256,256]{1,0:T(8,128)(2,1)S(1)} %copy-done.3, f32[1,256]{1,0:T(1,128)S(1)} %bitcast.8, bf16[512,256]{1,0:T(8,128)(2,1)S(1)} %copy-done.2, ...), custom_call_target="tpu_custom_call" | custom-call | tf_op jit(solution)/shard_map/pallas_call | solution.py:531
  84.4 0.7 copy.16
  85.1 0.8 copy.17
  85.9 0.7 copy.18
  (3 shorter events, 0.0 us)
Async XLA Ops:
  0.6 0.7 copy-start.8
  1.6 0.7 copy-start.9
  2.3 0.7 copy-start.6
  3.0 0.7 copy-start.7
  3.8 0.7 copy-start.5
  4.5 1.0 %copy-start = (f32[512,256]{1,0:T(8,128)S(1)}, f32[512,256]{1,0:T(8,128)}, u32[]{:S(2)}) copy-start(f32[512,256]{1,0:T(8,128)} %features.1) | copy-start | bytes 1572868
  5.6 1.0 %copy-start.1 = (bf16[1,16,1,128,128]{4,3,2,1,0:T(8,128)(2,1)S(1)}, bf16[1,16,1,128,128]{4,3,2,1,0:T(8,128)(2,1)}, u32[]{:S(2)}) copy-start(bf16[1,16,1,128,128]{4,3,2,1,0:T(8,128)(2,1)} %param.17) | copy-start | bytes 1572868
  6.6 0.9 %copy-start.2 = (bf16[512,256]{1,0:T(8,128)(2,1)S(1)}, bf16[512,256]{1,0:T(8,128)(2,1)}, u32[]{:S(2)}) copy-start(bf16[512,256]{1,0:T(8,128)(2,1)} %cotangent.1) | copy-start | bytes 786436
  7.6 0.9 %copy-start.3 = (bf16[256,256]{1,0:T(8,128)(2,1)S(1)}, bf16[256,256]{1,0:T(8,128)(2,1)}, u32[]{:S(2)}) copy-start(bf16[256,256]{1,0:T(8,128)(2,1)} %weight.1) | copy-start | bytes 393220
  8.5 0.9 %copy-start.4 = (bf16[4,128,128]{2,1,0:T(8,128)(2,1)S(1)}, bf16[4,128,128]{2,1,0:T(8,128)(2,1)}, u32[]{:S(2)}) copy-start(bf16[4,128,128]{2,1,0:T(8,128)(2,1)} %near_tiles.1) | copy-start | bytes 393220

commit v2 on v1

--- a/solution.py
+++ b/solution.py
@@ -152,15 +152,21 @@
     near_count,
     scale,
     flags,
+    features_hbm,
+    weight_hbm,
+    bias,
+    cotangent_hbm,
+    near_hbm,
+    far_hbm,
+    hidden,
+    grad_features,
+    weight_grad,
     features,
     weight,
-    bias,
     cotangent,
     near_tiles,
     far_tiles,
-    hidden,
-    grad_features,
-    weight_grad,
+    load_sem,
     own_feats,
     col_out,
     col_in,
@@ -198,6 +204,16 @@
     final_send,
     final_recv,
 ):
+    pairs = (
+        (features_hbm, features),
+        (near_hbm, near_tiles),
+        (far_hbm, far_tiles),
+        (weight_hbm, weight),
+        (cotangent_hbm, cotangent),
+    )
+    loads = [pltpu.make_async_copy(a, b, load_sem.at[i]) for i, (a, b) in enumerate(pairs)]
+    for load in loads:
+        load.start()
     f32, bf16 = jnp.float32, jnp.bfloat16
     dom, repl = lax.axis_index("dom"), lax.axis_index("repl")
     other = 1 - repl
@@ -244,6 +260,7 @@
         for c in range(blocks):
             col_out[k, c : c + 1] = jnp.full((1, half), far_col(k, c), f32)
     col_in[dom] = col_out[dom]
+    loads[0].wait()
     for h in range(2):
         own_feats[h] = features[:, h * half : (h + 1) * half].astype(bf16)
     pl.semaphore_wait(barrier, len(steps) + FAST_PLANE)
@@ -291,6 +308,8 @@
     for h in range(2):
         feat_in[h, pl.ds(pl.multiple_of(dom * tile, tile), tile)] = chosen(dom, h)
 
+    loads[1].wait()
+    loads[2].wait()
     for q in range(near_count):
         near_flip[q] = near_tiles[q].astype(f32).T.astype(bf16)
     for r in range(rows_dom):
@@ -331,6 +350,8 @@
         part_copy(h).wait_recv()
         summed[:, h * half : (h + 1) * half] = (part_own[h] + part_in[h].astype(f32)).astype(bf16)
 
+    loads[3].wait()
+    loads[4].wait()
     pre_act = jnp.dot(summed[...], weight[...], preferred_element_type=f32) + bias[...]
     sigma = 1.0 / (1.0 + jnp.exp(-pre_act))
     hidden[...] = (pre_act * sigma).astype(bf16)
@@ -527,6 +548,7 @@
     scale = 1.0 / math.sqrt(rows_dev * dom_count * 2)
     bf16, f32 = jnp.bfloat16, jnp.float32
     vmem = pl.BlockSpec(memory_space=pltpu.VMEM)
+    hbm = pl.BlockSpec(memory_space=pltpu.HBM)
     dma = pltpu.SemaphoreType.DMA
     return pl.pallas_call(
         functools.partial(layer_kernel, dom_count, near_count, scale),
@@ -535,9 +557,15 @@
             jax.ShapeDtypeStruct((rows_dev, feat), f32),
             jax.ShapeDtypeStruct((feat, feat), f32),
         ),
-        in_specs=[pl.BlockSpec(memory_space=pltpu.SMEM)] + [vmem] * 6,
+        in_specs=[pl.BlockSpec(memory_space=pltpu.SMEM)] + [hbm, hbm, vmem, hbm, hbm, hbm],
         out_specs=(vmem, vmem, vmem),
         scratch_shapes=[
+            pltpu.VMEM((rows_dev, feat), f32),
+            pltpu.VMEM((feat, feat), bf16),
+            pltpu.VMEM((rows_dev, feat), bf16),
+            pltpu.VMEM((near_count, tile, tile), bf16),
+            pltpu.VMEM((dom_count, tile, tile), bf16),
+            dma((5,)),
             pltpu.VMEM((2, rows_dev, half), bf16),
             pltpu.VMEM((dom_count, 8, half), f32),
             pltpu.VMEM((dom_count, 8, half), f32),
@@ -576,7 +604,7 @@
             dma((mates,)),
         ],
         compiler_params=pltpu.CompilerParams(
-            collective_id=0, has_side_effects=True, vmem_limit_bytes=40 * 1024 * 1024
+            collective_id=0, has_side_effects=True, vmem_limit_bytes=60 * 1024 * 1024
         ),
     )(
         flags,

time: 87 us -> 84.4 us (0.970)
  local copies, waits for them, and re-layouts: 10.4 us -> 6.31 us
  Pallas kernels: 75 us -> 76.1 us
    unnamed x23 -> x15, local copies, waits for them, and re-layouts: 9.98 us -> 5.87 us
    pallas_call x1, Pallas kernels: 75 us -> 76.1 us  [fused_on_device(): pl.pallas_call(functools.partial(layer_kernel, dom_count, near_count, sca...]
where the time goes in v2:
time: 84.4 us; the launch traced here: 84.2 us
  Pallas kernels  76.1 us (90%)
  local copies, waits for them, and re-layouts  6.31 us (7%)
  other arithmetic  1.06 us (1%)
    pallas_call x1, Pallas kernels, fused_on_device(): pl.pallas_call(functools.partial(layer_kernel, dom_count, near_count, sca...  76.1 us
    unnamed x15, local copies, waits for them, and re-layouts  5.87 us

profile of v2, /device:TPU:0, one launch (start us, length us, event | category | flops | bytes accessed | tf_op | source)
XLA Modules:
  0.0 84.2 jit_solution(2991402769277928680)
XLA Ops:
  0.6 0.0 copy-start.4
  0.6 0.6 copy-done.4
  1.3 0.1 slice_bitcast_fusion
  1.4 0.1 convert_reduce_fusion
  1.5 0.1 iota_compare_fusion.3
  1.6 0.0 copy-start.5
  1.6 0.1 convert_element_type.24
  1.6 0.6 copy-done.5
  2.2 0.1 iota_compare_fusion.2
  2.3 0.0 copy-start.2
  2.3 0.1 convert_element_type.25
  2.4 0.6 copy-done.2
  2.9 0.1 iota_compare_fusion.1
  3.0 0.0 copy-start.3
  3.0 0.1 convert_element_type.26
  3.1 0.6 copy-done.3
  3.7 0.1 iota_compare_fusion
  3.7 0.1 convert_element_type.27
  3.8 0.6 add_convert_fusion.flags
  4.5 76.1 %shard_map.121 = (bf16[512,256]{1,0:T(8,128)(2,1)}, f32[512,256]{1,0:T(8,128)}, f32[256,256]{1,0:T(8,128)}) custom-call(f32[240]{0:T(256)} %add_convert_fusion.flags, f32[512,256]{1,0:T(8,128)} %features_hbm.1, bf16[256,256]{1,0:T(8,128)(2,1)} %weight_hbm.1, f32[1,256]{1,0:T(1,128)} %bitcast.8, bf16[512,256]{1,0:T(8,128)(2,1)} %cotangent_hbm.1, ...), custom_call_target="tpu_custom_call" | custom-call | tf_op jit(solution)/shard_map/pallas_call | solution.py:553
  80.6 0.0 copy-start
  80.6 1.7 %copy.16 = bf16[512,256]{1,0:T(8,128)(2,1)} copy(bf16[512,256]{1,0:T(8,128)(2,1)} %get-tuple-element.6) | data formatting | bytes 524288
  82.4 0.0 copy-done
  82.4 0.0 copy-start.1
  82.4 0.8 copy.17
  83.2 0.3 copy-done.1
  83.4 0.7 copy.18
Async XLA Ops:
  0.6 0.7 copy-start.4
  1.6 0.7 copy-start.5
  2.3 0.7 copy-start.2
  3.0 0.7 copy-start.3
  80.6 1.7 %copy-start = (f32[512,256]{1,0:T(8,128)S(1)}, f32[512,256]{1,0:T(8,128)}, u32[]{:S(2)}) copy-start(f32[512,256]{1,0:T(8,128)} %get-tuple-element.7) | copy-start | bytes 1572868
  82.4 1.1 %copy-start.1 = (f32[256,256]{1,0:T(8,128)S(1)}, f32[256,256]{1,0:T(8,128)}, u32[]{:S(2)}) copy-start(f32[256,256]{1,0:T(8,128)} %get-tuple-element.8) | copy-start | bytes 786436
